TPU v7x, 32 devices: a whole 2x2x4 slice. The times are simulated.
32 devices in a mesh: seq: 4 (over y, x), head: 4 (over z), fsdp: 2 (over core).
Axes of the slice: x: 2, y: 2, z: 4, core: 2. Of those that a mesh axis runs over, the one named last changes fastest.
Arguments:
- query: bfloat16 [2, 512, 1024], P('fsdp', 'seq', 'head'), may hold values from -6 to 6
- keys: bfloat16 [2, 512, 1024], P('fsdp', 'seq', 'head'), may hold values from -6 to 6
- values: bfloat16 [2, 512, 1024], P('fsdp', 'seq', 'head'), may hold values from -6 to 6
- grad_out: bfloat16 [2, 512, 4096], P('fsdp', 'seq'), may hold values from -6 to 6
- w_out: bfloat16 [1024, 4096], P('head', 'fsdp'), may hold values from -0.1875 to 0.1875
- link_flags: int32 [4, 2], P('seq'), may hold values 0 or 1
Outputs:
- grad_query: bfloat16 [2, 512, 1024], P('fsdp', 'seq', 'head')
- grad_keys: bfloat16 [2, 512, 1024], P('fsdp', 'seq', 'head')
- grad_values: bfloat16 [2, 512, 1024], P('fsdp', 'seq', 'head')
- grad_w_out_t: float32 [4096, 1024], P('seq', ('head', 'fsdp'))
All inputs are finite; a program needn't handle non-finite values. No bound on the sum of `link_flags` on one device may be relied on, other than what follows from the above.
Results may differ from a plain program's by a relative error of at most 0.01.
Values may be sent and summed in bfloat16 or wider, within the bound.
A program may use at most 64 MiB of HBM per device.

v0:
```python
import math

import jax
import jax.numpy as jnp
from jax import lax
from jax.sharding import PartitionSpec as P

D = 4096
HD = 128


def swapped(shard, axis, distance):
    return lax.ppermute(shard, axis, [(i, i ^ 1 << distance) for i in range(lax.axis_size(axis))])


def per_device(query, keys, values, grad_out, w_out, link_flags):
    local_seqs, block_len, local_width = query.shape
    local_heads = local_width // HD
    levels = lax.axis_size("seq").bit_length() - 1
    score_scale = 1.0 / math.sqrt(HD)
    key_value = jnp.stack([keys, values])
    collected = [key_value]
    for level in range(levels):
        collected.append(swapped(key_value, "seq", level))
    slots = levels + 1
    near_all = jnp.stack(collected).reshape(slots, 2, local_seqs, block_len, local_heads, HD)
    key_near = near_all[:, 0]
    value_near = near_all[:, 1]
    query_heads = query.reshape(local_seqs, block_len, local_heads, HD)
    spots = jnp.arange(block_len, dtype=jnp.int32)
    causal = spots[None, :] <= spots[:, None]
    link_on = jnp.concatenate([jnp.ones((1,), dtype=bool), link_flags[0] > 0])
    first_slot = jnp.arange(slots, dtype=jnp.int32) == 0
    allowed = jnp.where(first_slot[None, :, None], causal[:, None, :], link_on[None, :, None])
    scores = (
        jnp.einsum("sthc,msuhc->shtmu", query_heads, key_near, preferred_element_type=jnp.float32)
        * score_scale
    )
    scores = jnp.where(allowed[None, None], scores, -jnp.inf)
    row_max = jnp.max(scores, axis=(3, 4), keepdims=True)
    raw = jnp.exp(scores - row_max)
    softmax = raw / jnp.sum(raw, axis=(3, 4), keepdims=True)
    probs_low = softmax.astype(jnp.bfloat16)
    attended = jnp.einsum(
        "shtmu,msuhc->sthc", probs_low, value_near, preferred_element_type=jnp.float32
    ).astype(jnp.bfloat16)
    grad_rows = grad_out.reshape(local_seqs * block_len, D)
    columns = grad_rows
    grad_att = lax.dot_general(
        columns,
        lax.all_gather(w_out, "fsdp", axis=1, tiled=True),
        (((1,), (1,)), ((), ())),
        preferred_element_type=jnp.float32,
    ).astype(jnp.bfloat16)
    grad_heads = grad_att.reshape(local_seqs, block_len, local_heads, HD)
    attended_rows = attended.reshape(local_seqs * block_len, local_width)
    columns = grad_rows
    seq_share = lax.psum_scatter(
        lax.dot_general(
            columns, attended_rows, (((0,), (0,)), ((), ())), preferred_element_type=jnp.float32
        ),
        "seq",
        scatter_dimension=0,
        tiled=True,
    )
    grad_w = lax.psum_scatter(
        seq_share.astype(jnp.bfloat16), "fsdp", scatter_dimension=1, tiled=True
    ).astype(jnp.float32)
    grad_probs = jnp.einsum(
        "sthc,msuhc->shtmu", grad_heads, value_near, preferred_element_type=jnp.float32
    )
    row_dot = jnp.sum(softmax * grad_probs, axis=(3, 4), keepdims=True)
    grad_scores = (softmax * (grad_probs - row_dot) * score_scale).astype(jnp.bfloat16)
    grad_query = jnp.einsum(
        "shtmu,msuhc->sthc", grad_scores, key_near, preferred_element_type=jnp.float32
    ).astype(jnp.bfloat16)
    key_terms = jnp.einsum(
        "shtmu,sthc->msuhc", grad_scores, query_heads, preferred_element_type=jnp.float32
    )
    value_terms = jnp.einsum(
        "shtmu,sthc->msuhc", probs_low, grad_heads, preferred_element_type=jnp.float32
    )
    grad_key = key_terms[0]
    grad_value = value_terms[0]
    for level in range(levels):
        outgoing = jnp.stack([key_terms[level + 1], value_terms[level + 1]]).astype(jnp.bfloat16)
        returned = swapped(outgoing, "seq", level)
        grad_key = grad_key + returned[0].astype(jnp.float32)
        grad_value = grad_value + returned[1].astype(jnp.float32)
    shape_out = (local_seqs, block_len, local_width)
    return (
        grad_query.reshape(shape_out),
        grad_key.astype(jnp.bfloat16).reshape(shape_out),
        grad_value.astype(jnp.bfloat16).reshape(shape_out),
        grad_w,
    )


def solution(mesh):
    in_specs = (
        P("fsdp", "seq", "head"),
        P("fsdp", "seq", "head"),
        P("fsdp", "seq", "head"),
        P("fsdp", "seq", None),
        P("head", "fsdp"),
        P("seq", None),
    )
    out_specs = (
        P("fsdp", "seq", "head"),
        P("fsdp", "seq", "head"),
        P("fsdp", "seq", "head"),
        P("seq", ("head", "fsdp")),
    )
    return jax.shard_map(
        per_device, mesh=mesh, in_specs=in_specs, out_specs=out_specs, check_vma=False
    )
```

profile of v0, /device:TPU:1, one launch (start us, length us, event | category | flops | bytes accessed | tf_op | source)
XLA Modules:
  0.0 94.4 jit_solution(9334522719291881944)
XLA Ops:
  8.1 0.7 all-gather.2.cloned.1.call-update
  8.8 0.9 %copy.24 = bf16[1,128,256]{1,2,0:T(8,128)(2,1)S(1)} copy(bf16[1,128,256]{2,1,0:T(8,128)(2,1)} %param.7) | data formatting | bytes 131072 | tf_op args[1]
  9.8 1.0 %copy.25 = bf16[1,128,256]{1,2,0:T(8,128)(2,1)S(1)} copy(bf16[1,128,256]{2,1,0:T(8,128)(2,1)} %param.8) | data formatting | bytes 131072 | tf_op args[2]
  10.7 2.1 %collective-permute-start.1 = (bf16[2,1,128,256]{2,3,0,1:T(8,128)(2,1)S(1)}, bf16[2,1,128,256]{2,3,0,1:T(8,128)(2,1)S(1)}, u32[]{:S(2)}, u32[]{:S(2)}) collective-permute-start(bf16[2,1,128,256]{2,3,0,1:T(8,128)(2,1)S(1)} %pad_maximum_fusion.1), channel_id=1, source_target_pairs={{0,16},{8,24},{16,0},{24,8},{1,17},{9,25},{17,1},{25,9},{2,18},{10... | collective-permute-start | bytes 393224 | tf_op jit(solution)/shard_map/ppermute | solution.py:13
  12.9 1.2 %collective-permute-start = (bf16[2,1,128,256]{2,3,0,1:T(8,128)(2,1)S(1)}, bf16[2,1,128,256]{2,3,0,1:T(8,128)(2,1)S(1)}, u32[]{:S(2)}, u32[]{:S(2)}) collective-permute-start(bf16[2,1,128,256]{2,3,0,1:T(8,128)(2,1)S(1)} %pad_maximum_fusion.1), channel_id=1, source_target_pairs={{0,8},{8,0},{16,24},{24,16},{1,9},{9,1},{17,25},{25,17},{2,10},{10... | collective-permute-start | bytes 393224 | tf_op jit(solution)/shard_map/ppermute | solution.py:13
  14.4 0.9 reshape.280
  15.6 0.5 collective-permute-done.1
  16.2 0.7 collective-permute-done
  17.4 0.3 fusion.3
  17.7 2.7 %convolution_bitcast_fusion = f32[4096,256]{0,1:T(8,128)} fusion(bf16[128,256]{0,1:T(8,128)(2,1)S(1)} %bitcast.96, bf16[1,128,4096]{2,1,0:T(8,128)(2,1)S(1)} %copy-done), kind=kOutput, calls=%fused_computation | convolution fusion | flops 268435456 | bytes 5308416 | tf_op jit(solution)/shard_map/dot_general | solution.py:59
  20.5 3.0 %all-gather.2.cloned.1.call-done = bf16[256,4096]{1,0:T(8,128)(2,1)} async-done(((bf16[256,2048]{1,0:T(8,128)(2,1)}), bf16[256,4096]{1,0:T(8,128)(2,1)}) %all-gather.2.cloned.1.call-update) | async-done | bytes 2097168 | tf_op jit(solution)/shard_map/all_gather | solution.py:51
  23.5 2.4 %convolution_convert_fusion = bf16[128,256]{1,0:T(8,128)(2,1)S(1)} fusion(bf16[256,4096]{1,0:T(8,128)(2,1)} %all-gather.2.cloned.1.call-done, bf16[1,128,4096]{2,1,0:T(8,128)(2,1)S(1)} %copy-done), kind=kOutput, calls=%fused_computation.8 | convolution fusion | flops 268468224 | bytes 3211264 | tf_op jit(solution)/shard_map/dot_general | solution.py:49
  26.6 0.3 fusion.25
  26.9 47.6 %reduce-scatter.3.cloned.1.call-done = f32[1024,256]{0,1:T(8,128)} async-done(((f32[4096,256]{0,1:T(8,128)}), f32[1024,256]{0,1:T(8,128)}) %reduce-scatter.3.cloned.1.call-update) | async-done | bytes 1048592 | tf_op jit(solution)/shard_map/reduce_scatter | solution.py:58
  74.5 2.1 %convert_element_type.152 = bf16[1024,256]{0,1:T(8,128)(2,1)} convert(f32[1024,256]{0,1:T(8,128)} %reduce-scatter.3.cloned.1.call-done) | non-fusion elementwise | flops 262144 | bytes 1572864 | tf_op jit(solution)/shard_map/convert_element_type | solution.py:67
  76.6 1.1 %collective-permute-start.3 = (bf16[2,1,128,2,128]{2,4,0,3,1:T(8,128)(2,1)S(1)}, bf16[2,1,128,2,128]{2,4,0,3,1:T(8,128)(2,1)S(1)}, u32[]{:S(2)}, u32[]{:S(2)}) collective-permute-start(bf16[2,1,128,2,128]{2,4,0,3,1:T(8,128)(2,1)S(1)} %pad_maximum_fusion.3), channel_id=1, source_target_pairs={{0,16},{8,24},{16,0},{24,8},{1,17},{9,25},{17,1},{25,9},{2,18},{10... | collective-permute-start | bytes 393224 | tf_op jit(solution)/shard_map/ppermute | solution.py:13
  77.8 0.4 collective-permute-start.2
  78.5 0.7 copy.42
  79.2 1.7 %collective-permute-done.3 = bf16[2,1,128,2,128]{2,4,0,3,1:T(8,128)(2,1)S(1)} collective-permute-done((bf16[2,1,128,2,128]{2,4,0,3,1:T(8,128)(2,1)S(1)}, bf16[2,1,128,2,128]{2,4,0,3,1:T(8,128)(2,1)S(1)}, u32[]{:S(2)}, u32[]{:S(2)}) %collective-permute-start.3) | collective-permute-done | bytes 131104 | tf_op jit(solution)/shard_map/ppermute | solution.py:13
  81.0 1.0 %collective-permute-done.2 = bf16[2,1,128,2,128]{2,4,0,3,1:T(8,128)(2,1)S(1)} collective-permute-done((bf16[2,1,128,2,128]{2,4,0,3,1:T(8,128)(2,1)S(1)}, bf16[2,1,128,2,128]{2,4,0,3,1:T(8,128)(2,1)S(1)}, u32[]{:S(2)}, u32[]{:S(2)}) %collective-permute-start.2) | collective-permute-done | bytes 131104 | tf_op jit(solution)/shard_map/ppermute | solution.py:13
  82.0 0.7 copy.44
  82.8 0.7 copy.43
  83.5 1.6 %reduce-scatter.5.cloned.1.call-done = bf16[1024,128]{0,1:T(8,128)(2,1)} async-done(((bf16[1024,256]{0,1:T(8,128)(2,1)}), bf16[1024,128]{0,1:T(8,128)(2,1)}) %reduce-scatter.5.cloned.1.call-update) | async-done | bytes 262160 | tf_op jit(solution)/shard_map/reduce_scatter | solution.py:66
  85.1 1.9 %copy.45 = f32[1024,128]{1,0:T(8,128)} copy(bf16[1024,128]{0,1:T(8,128)(2,1)} %reduce-scatter.5.cloned.1.call-done) | data formatting | bytes 786432
  (39 shorter events, 2.4 us)
Async XLA Ops:
  8.0 9.7 %copy-start = (bf16[1,128,4096]{2,1,0:T(8,128)(2,1)S(1)}, bf16[1,128,4096]{2,1,0:T(8,128)(2,1)}, u32[]{:S(2)}) copy-start(bf16[1,128,4096]{2,1,0:T(8,128)(2,1)} %param.9) | copy-start | bytes 3145732
  8.0 7.3 %copy-start.3 = (s32[1,2]{1,0:T(1,128)S(1)}, s32[1,2]{1,0:T(1,128)}, u32[]{:S(2)}) copy-start(s32[1,2]{1,0:T(1,128)} %param.11) | copy-start | bytes 28
  8.0 15.5 %all-gather.2.cloned.1.call-start = ((), (), s32[]{:S(2)}) async-start(), calls=%async_computation.2 | async-start | bytes 3145728 | tf_op jit(solution)/shard_map/all_gather | solution.py:51
  8.8 65.7 %reduce-scatter.3.cloned.1.call-start = ((), (), s32[]{:S(2)}) async-start(), calls=%async_computation.3 | async-start | bytes 5242880 | tf_op jit(solution)/shard_map/reduce_scatter | solution.py:58
  10.7 5.4 %collective-permute-start.1 = (bf16[2,1,128,256]{2,3,0,1:T(8,128)(2,1)S(1)}, bf16[2,1,128,256]{2,3,0,1:T(8,128)(2,1)S(1)}, u32[]{:S(2)}, u32[]{:S(2)}) collective-permute-start(bf16[2,1,128,256]{2,3,0,1:T(8,128)(2,1)S(1)} %pad_maximum_fusion.1), channel_id=1, source_target_pairs={{0,16},{8,24},{16,0},{24,8},{1,17},{9,25},{17,1},{25,9},{2,18},{10... | collective-permute-start | bytes 393224 | tf_op jit(solution)/shard_map/ppermute | solution.py:13
  12.9 4.1 %collective-permute-start = (bf16[2,1,128,256]{2,3,0,1:T(8,128)(2,1)S(1)}, bf16[2,1,128,256]{2,3,0,1:T(8,128)(2,1)S(1)}, u32[]{:S(2)}, u32[]{:S(2)}) collective-permute-start(bf16[2,1,128,256]{2,3,0,1:T(8,128)(2,1)S(1)} %pad_maximum_fusion.1), channel_id=1, source_target_pairs={{0,8},{8,0},{16,24},{24,16},{1,9},{9,1},{17,25},{25,17},{2,10},{10... | collective-permute-start | bytes 393224 | tf_op jit(solution)/shard_map/ppermute | solution.py:13
  17.1 3.3 %copy-start.1 = (bf16[3,2,1,128,2,128]{5,3,0,4,2,1:T(8,128)(2,1)}, bf16[3,2,1,128,2,128]{5,3,0,4,2,1:T(8,128)(2,1)S(1)}, u32[]{:S(2)}) copy-start(bf16[3,2,1,128,2,128]{5,3,0,4,2,1:T(8,128)(2,1)S(1)} %pad_maximum_fusion) | copy-start | bytes 1179652
  20.4 64.7 %reduce-scatter.5.cloned.1.call-start = ((), (), s32[]{:S(2)}) async-start(), calls=%async_computation.4 | async-start | bytes 786432 | tf_op jit(solution)/shard_map/reduce_scatter | solution.py:66
  20.4 5.5 %slice-start = ((bf16[3,2,1,128,2,128]{5,3,0,4,2,1:T(8,128)(2,1)}), bf16[3,1,1,128,2,128]{5,3,0,4,2,1:T(8,128)(2,1)S(1)}, s32[]{:S(2)}) async-start(bf16[3,2,1,128,2,128]{5,3,0,4,2,1:T(8,128)(2,1)} %copy-done.1), calls=%async_computation.5 | async-start | bytes 393216 | tf_op jit(solution)/shard_map/slice | solution.py:28
  26.6 51.6 %copy-start.2 = (bf16[3,2,1,128,2,128]{5,3,0,4,2,1:T(8,128)(2,1)S(1)}, bf16[3,2,1,128,2,128]{5,3,0,4,2,1:T(8,128)(2,1)}, u32[]{:S(2)}) copy-start(bf16[3,2,1,128,2,128]{5,3,0,4,2,1:T(8,128)(2,1)} %copy-done.1) | copy-start | bytes 1179652
  76.6 4.3 %collective-permute-start.3 = (bf16[2,1,128,2,128]{2,4,0,3,1:T(8,128)(2,1)S(1)}, bf16[2,1,128,2,128]{2,4,0,3,1:T(8,128)(2,1)S(1)}, u32[]{:S(2)}, u32[]{:S(2)}) collective-permute-start(bf16[2,1,128,2,128]{2,4,0,3,1:T(8,128)(2,1)S(1)} %pad_maximum_fusion.3), channel_id=1, source_target_pairs={{0,16},{8,24},{16,0},{24,8},{1,17},{9,25},{17,1},{25,9},{2,18},{10... | collective-permute-start | bytes 393224 | tf_op jit(solution)/shard_map/ppermute | solution.py:13
  77.8 4.2 %collective-permute-start.2 = (bf16[2,1,128,2,128]{2,4,0,3,1:T(8,128)(2,1)S(1)}, bf16[2,1,128,2,128]{2,4,0,3,1:T(8,128)(2,1)S(1)}, u32[]{:S(2)}, u32[]{:S(2)}) collective-permute-start(bf16[2,1,128,2,128]{2,4,0,3,1:T(8,128)(2,1)S(1)} %pad_maximum_fusion.2), channel_id=1, source_target_pairs={{0,8},{8,0},{16,24},{24,16},{1,9},{9,1},{17,25},{25,17},{2,10},{10... | collective-permute-start | bytes 393224 | tf_op jit(solution)/shard_map/ppermute | solution.py:13
Sparse Core Ops, SparseCore 0:
  10.4 13.0 all-gather.1
  76.7 8.3 reduce-scatter.4
Sparse Core Ops, SparseCore 1:
  20.5 53.9 reduce-scatter.2
where the time goes:
time: 95 us; the launch traced here: 94.4 us
  waiting for transfers between devices  56.9 us (60%)
  between operations  15.7 us (17%)
  local copies, waits for them, and re-layouts  7.57 us (8%)
  matrix products  6.49 us (7%)
  starting transfers between devices  5.04 us (5%)
  other arithmetic  2.74 us (3%)
    reduce_scatter x1, waiting for transfers between devices, per_device(): lax.psum_scatter(lax.dot_general(columns, attended_rows, (((0,), (0,)), (...  47.6 us
    unnamed x14, local copies, waits for them, and re-layouts  6.03 us
    ppermute x4, starting transfers between devices, swapped(): lax.ppermute(shard, axis, [(i, i ^ 1 << distance) for i in range(lax.axis...  4.92 us
    ppermute x4, waiting for transfers between devices, swapped(): lax.ppermute(shard, axis, [(i, i ^ 1 << distance) for i in range(lax.axis...  3.97 us
    all_gather x1, waiting for transfers between devices, per_device(): lax.all_gather(w_out, 'fsdp', axis=1, tiled=True)  3.03 us
    dot_general x1, matrix products, per_device(): lax.dot_general(columns, attended_rows, (((0,), (0,)), ((), ())), preferr...  2.65 us
    dot_general x1, matrix products, per_device(): lax.dot_general(columns, lax.all_gather(w_out, 'fsdp', axis=1, tiled=True...  2.42 us
    convert_element_type x1, other arithmetic, per_device(): seq_share.astype(jnp.bfloat16)  2.09 us
  transfers between devices with their start and end apart: 7, of which 7 were waited for; matrix products, arithmetic and copies ran while one was open for 14% of the time, Pallas kernels for 0%

commit v1 on v0

--- a/solution.py
+++ b/solution.py
@@ -1,8 +1,11 @@
+import functools
 import math
 
 import jax
 import jax.numpy as jnp
 from jax import lax
+from jax.experimental import pallas as pl
+from jax.experimental.pallas import tpu as pltpu
 from jax.sharding import PartitionSpec as P
 
 D = 4096
@@ -13,7 +16,7 @@
     return lax.ppermute(shard, axis, [(i, i ^ 1 << distance) for i in range(lax.axis_size(axis))])
 
 
-def per_device(query, keys, values, grad_out, w_out, link_flags):
+def plain_device(query, keys, values, grad_out, w_out, link_flags):
     local_seqs, block_len, local_width = query.shape
     local_heads = local_width // HD
     levels = lax.axis_size("seq").bit_length() - 1
@@ -96,6 +99,311 @@
     )
 
 
+def contract(a, b, dims):
+    return lax.dot_general(a, b, (dims, ((), ())), preferred_element_type=jnp.float32)
+
+
+def fused_kernel(
+    n_seq,
+    flags_ref,
+    query_hbm,
+    keys_hbm,
+    values_hbm,
+    go_hbm,
+    w_hbm,
+    gq_ref,
+    gk_ref,
+    gv_ref,
+    gw_ref,
+    q_buf,
+    k_all,
+    v_all,
+    go_buf,
+    w_all,
+    go_all,
+    att_all,
+    term_send,
+    term_recv,
+    gk_acc,
+    gv_acc,
+    part_send,
+    part_recv,
+    local_sem,
+    kv_send_sem,
+    kv_recv_sem,
+    w_sem,
+    go_send_sem,
+    go_recv_sem,
+    att_send_sem,
+    att_recv_sem,
+    term_send_sem,
+    term_recv_sem,
+    part_send_sem,
+    part_recv_sem,
+):
+    levels = n_seq.bit_length() - 1
+    block, width = q_buf.shape
+    heads = width // HD
+    rows = go_all.shape[1]
+    half_d = w_hbm.shape[1]
+    half_w = width // 2
+    scale = 1.0 / math.sqrt(HD)
+    me = lax.axis_index("seq")
+    core = lax.axis_index("fsdp")
+    other = 1 - core
+
+    def peer(mask):
+        out = me
+        for bit in range(levels):
+            if mask >> bit & 1:
+                out = out + (1 << bit) * (1 - 2 * (lax.div(me, 1 << bit) % 2))
+        return out
+
+    def remote(src, dst, send, recv, target):
+        return pltpu.make_async_remote_copy(
+            src_ref=src,
+            dst_ref=dst,
+            send_sem=send,
+            recv_sem=recv,
+            device_id=target,
+            device_id_type=pl.DeviceIdType.MESH,
+        )
+
+    locals_ = [
+        pltpu.make_async_copy(query_hbm, q_buf, local_sem.at[0]),
+        pltpu.make_async_copy(keys_hbm, k_all.at[pl.ds(0, block)], local_sem.at[1]),
+        pltpu.make_async_copy(values_hbm, v_all.at[pl.ds(0, block)], local_sem.at[2]),
+        pltpu.make_async_copy(go_hbm, go_buf, local_sem.at[3]),
+        pltpu.make_async_copy(w_hbm, w_all.at[0], local_sem.at[4]),
+    ]
+    for copy in locals_:
+        copy.start()
+
+    barrier = pltpu.get_barrier_semaphore()
+    for mask in range(1, n_seq):
+        pl.semaphore_signal(
+            barrier, inc=1, device_id={"seq": peer(mask)}, device_id_type=pl.DeviceIdType.MESH
+        )
+    pl.semaphore_signal(
+        barrier, inc=1, device_id={"fsdp": other}, device_id_type=pl.DeviceIdType.MESH
+    )
+    pl.semaphore_wait(barrier, n_seq)
+
+    kv_copies = []
+    for level in range(levels):
+        spot = pl.ds((level + 1) * block, block)
+        for which, (src, dst) in enumerate(((keys_hbm, k_all), (values_hbm, v_all))):
+            i = 2 * level + which
+            kv_copies.append(
+                remote(
+                    src,
+                    dst.at[spot],
+                    kv_send_sem.at[i],
+                    kv_recv_sem.at[i],
+                    {"seq": peer(1 << level)},
+                )
+            )
+    for copy in kv_copies:
+        copy.start()
+    w_copy = remote(w_hbm, w_all.at[1], w_sem.at[0], w_sem.at[1], {"fsdp": other})
+    w_copy.start()
+    go_copies = []
+    for mask in range(1, n_seq):
+        target = peer(mask)
+        columns = pl.ds(pl.multiple_of(target * rows, 128), rows)
+        go_copies.append(
+            remote(
+                go_hbm.at[:, columns],
+                go_all.at[pl.ds(mask * block, block)],
+                go_send_sem.at[mask - 1],
+                go_recv_sem.at[mask - 1],
+                {"seq": target},
+            )
+        )
+    for copy in go_copies:
+        copy.start()
+
+    locals_[3].wait()
+    locals_[4].wait()
+    own_columns = pl.ds(pl.multiple_of(core * half_d, 128), half_d)
+    other_columns = pl.ds(pl.multiple_of(other * half_d, 128), half_d)
+    grad_att = contract(go_buf[:, own_columns], w_all[0], ((1,), (1,)))
+    go_all[pl.ds(0, block), :] = go_buf[:, pl.ds(pl.multiple_of(me * rows, 128), rows)]
+
+    for copy in locals_[:3]:
+        copy.wait()
+    for copy in kv_copies:
+        copy.wait_recv()
+
+    spots_t = lax.broadcasted_iota(jnp.int32, (block, block), 0)
+    spots_u = lax.broadcasted_iota(jnp.int32, (block, block), 1)
+    allowed = [spots_u <= spots_t]
+    for level in range(levels):
+        allowed.append(jnp.full((block, block), flags_ref[0, level], jnp.int32) > 0)
+    allowed = jnp.concatenate(allowed, axis=1)
+
+    softmaxes = []
+    lows = []
+    for h in range(heads):
+        cols = slice(h * HD, (h + 1) * HD)
+        scores = contract(q_buf[:, cols], k_all[:, cols], ((1,), (1,))) * scale
+        scores = jnp.where(allowed, scores, -jnp.inf)
+        raw = jnp.exp(scores - jnp.max(scores, axis=1, keepdims=True))
+        softmax = raw / jnp.sum(raw, axis=1, keepdims=True)
+        low = softmax.astype(jnp.bfloat16)
+        att_all[pl.ds(0, block), cols] = contract(low, v_all[:, cols], ((1,), (0,))).astype(
+            jnp.bfloat16
+        )
+        softmaxes.append(softmax)
+        lows.append(low)
+
+    att_copies = []
+    for mask in range(1, n_seq):
+        att_copies.append(
+            remote(
+                att_all.at[pl.ds(0, block)],
+                att_all.at[pl.ds(mask * block, block)],
+                att_send_sem.at[mask - 1],
+                att_recv_sem.at[mask - 1],
+                {"seq": peer(mask)},
+            )
+        )
+    for copy in att_copies:
+        copy.start()
+
+    w_copy.wait_recv()
+    grad_att = grad_att + contract(go_buf[:, other_columns], w_all[1], ((1,), (1,)))
+    grad_att = grad_att.astype(jnp.bfloat16)
+
+    for h in range(heads):
+        cols = slice(h * HD, (h + 1) * HD)
+        grad_head = grad_att[:, cols]
+        grad_probs = contract(grad_head, v_all[:, cols], ((1,), (1,)))
+        row_dot = jnp.sum(softmaxes[h] * grad_probs, axis=1, keepdims=True)
+        grad_scores = (softmaxes[h] * (grad_probs - row_dot) * scale).astype(jnp.bfloat16)
+        key_terms = contract(grad_scores, q_buf[:, cols], ((0,), (0,)))
+        value_terms = contract(lows[h], grad_head, ((0,), (0,)))
+        gk_acc[:, cols] = key_terms[:block]
+        gv_acc[:, cols] = value_terms[:block]
+        for level in range(levels):
+            part = slice((level + 1) * block, (level + 2) * block)
+            term_send[level, 0, :, cols] = key_terms[part].astype(jnp.bfloat16)
+            term_send[level, 1, :, cols] = value_terms[part].astype(jnp.bfloat16)
+        gq_ref[:, cols] = contract(grad_scores, k_all[:, cols], ((1,), (0,))).astype(jnp.bfloat16)
+
+    term_copies = []
+    for level in range(levels):
+        term_copies.append(
+            remote(
+                term_send.at[level],
+                term_recv.at[level],
+                term_send_sem.at[level],
+                term_recv_sem.at[level],
+                {"seq": peer(1 << level)},
+            )
+        )
+    for copy in term_copies:
+        copy.start()
+
+    for copy in go_copies:
+        copy.wait_recv()
+    for copy in att_copies:
+        copy.wait_recv()
+    chunks = part_send.shape[0]
+    step = rows // chunks
+    part_copies = []
+    for i in range(chunks):
+        span = slice(i * step, (i + 1) * step)
+        product = contract(go_all[:, span], att_all[...], ((0,), (0,)))
+        low_half, high_half = product[:, :half_w], product[:, half_w:]
+        part_send[i] = jnp.where(core == 0, high_half, low_half).astype(jnp.bfloat16)
+        copy = remote(
+            part_send.at[i],
+            part_recv.at[i],
+            part_send_sem.at[i],
+            part_recv_sem.at[i],
+            {"fsdp": other},
+        )
+        copy.start()
+        part_copies.append(copy)
+        gw_ref[span, :] = jnp.where(core == 0, low_half, high_half)
+
+    for copy in term_copies:
+        copy.wait_recv()
+    grad_key = gk_acc[...]
+    grad_value = gv_acc[...]
+    for level in range(levels):
+        grad_key = grad_key + term_recv[level, 0].astype(jnp.float32)
+        grad_value = grad_value + term_recv[level, 1].astype(jnp.float32)
+    gk_ref[...] = grad_key.astype(jnp.bfloat16)
+    gv_ref[...] = grad_value.astype(jnp.bfloat16)
+
+    for i, copy in enumerate(part_copies):
+        span = slice(i * step, (i + 1) * step)
+        copy.wait_recv()
+        gw_ref[span, :] = gw_ref[span, :] + part_recv[i].astype(jnp.float32)
+    for copy in kv_copies + [w_copy] + go_copies + att_copies + term_copies + part_copies:
+        copy.wait_send()
+
+
+def fused_device(n_seq, query, keys, values, grad_out, w_out, link_flags):
+    _, block, width = query.shape
+    levels = n_seq.bit_length() - 1
+    rows = D // n_seq
+    chunks = 4
+    shape = (block, width)
+    half_w = width // 2
+    vmem = pl.BlockSpec(memory_space=pltpu.VMEM)
+    anywhere = pl.BlockSpec(memory_space=pl.ANY)
+    bf16 = jnp.bfloat16
+    dma = pltpu.SemaphoreType.DMA
+    outs = pl.pallas_call(
+        functools.partial(fused_kernel, n_seq),
+        out_shape=[jax.ShapeDtypeStruct(shape, bf16)] * 3
+        + [jax.ShapeDtypeStruct((rows, half_w), jnp.float32)],
+        in_specs=[pl.BlockSpec(memory_space=pltpu.SMEM)] + [anywhere] * 5,
+        out_specs=[vmem] * 4,
+        scratch_shapes=[
+            pltpu.VMEM(shape, bf16),
+            pltpu.VMEM(((levels + 1) * block, width), bf16),
+            pltpu.VMEM(((levels + 1) * block, width), bf16),
+            pltpu.VMEM((block, D), bf16),
+            pltpu.VMEM((2,) + w_out.shape, bf16),
+            pltpu.VMEM((n_seq * block, rows), bf16),
+            pltpu.VMEM((n_seq * block, width), bf16),
+            pltpu.VMEM((levels, 2) + shape, bf16),
+            pltpu.VMEM((levels, 2) + shape, bf16),
+            pltpu.VMEM(shape, jnp.float32),
+            pltpu.VMEM(shape, jnp.float32),
+            pltpu.VMEM((chunks, rows // chunks, half_w), bf16),
+            pltpu.VMEM((chunks, rows // chunks, half_w), bf16),
+            dma((5,)),
+            dma((2 * levels,)),
+            dma((2 * levels,)),
+            dma((2,)),
+            dma((n_seq - 1,)),
+            dma((n_seq - 1,)),
+            dma((n_seq - 1,)),
+            dma((n_seq - 1,)),
+            dma((levels,)),
+            dma((levels,)),
+            dma((chunks,)),
+            dma((chunks,)),
+        ],
+        compiler_params=pltpu.CompilerParams(
+            collective_id=0, has_side_effects=True, vmem_limit_bytes=40 * 1024 * 1024
+        ),
+    )(link_flags, query[0], keys[0], values[0], grad_out[0], w_out)
+    return outs[0][None], outs[1][None], outs[2][None], outs[3]
+
+
+def per_device(n_seq, query, keys, values, grad_out, w_out, link_flags):
+    args = (query, keys, values, grad_out, w_out, link_flags)
+    if query.shape[0] == 1 and (D // n_seq) % 512 == 0 and query.shape[2] == 2 * HD:
+        return fused_device(n_seq, *args)
+    return plain_device(*args)
+
+
 def solution(mesh):
     in_specs = (
         P("fsdp", "seq", "head"),
@@ -112,5 +420,5 @@
         P("seq", ("head", "fsdp")),
     )
     return jax.shard_map(
-        per_device, mesh=mesh, in_specs=in_specs, out_specs=out_specs, check_vma=False
-    )
+        functools.partial(per_device, mesh.shape["seq"]), mesh=mesh, in_specs=in_specs, out_specs=out_specs, check_vma=False
+    )

time: 95 us -> 35.6 us (0.37)
  waiting for transfers between devices: 56.9 us -> 0 us
  Pallas kernels: 0 us -> 26.3 us
  between operations: 15.7 us -> 0.66 us
  matrix products: 6.49 us -> 0 us
  starting transfers between devices: 5.04 us -> 0 us
  other arithmetic: 2.74 us -> 0 us
    reduce_scatter x2 -> x0, waiting for transfers between devices: 49.2 us -> none  [the longest x1 47.6 us: per_device(): lax.psum_scatter(lax.dot_general(columns, attended_rows, (((0,), (0,)), (...]
    pallas_call x0 -> x1, Pallas kernels: none -> 26.3 us  [fused_device(): pl.pallas_call(functools.partial(fused_kernel, n_seq), out_shape=[jax.Sha...]
    dot_general x7 -> x0, matrix products: 6.28 us -> none  [the longest x1 2.65 us: per_device(): lax.dot_general(columns, attended_rows, (((0,), (0,)), ((), ())), preferr...]
    ppermute x4 -> x0, starting transfers between devices: 4.92 us -> none  [swapped(): lax.ppermute(shard, axis, [(i, i ^ 1 << distance) for i in range(lax.axis...]
    ppermute x4 -> x0, waiting for transfers between devices: 3.97 us -> none  [swapped(): lax.ppermute(shard, axis, [(i, i ^ 1 << distance) for i in range(lax.axis...]
    all_gather x1 -> x0, waiting for transfers between devices: 3.03 us -> none  [per_device(): lax.all_gather(w_out, 'fsdp', axis=1, tiled=True)]
    convert_element_type x3 -> x0, other arithmetic: 2.27 us -> none  [the longest x1 2.09 us: per_device(): seq_share.astype(jnp.bfloat16)]
    unnamed x14 -> x16, local copies, waits for them, and re-layouts: 6.03 us -> 8.3 us
  transfers between devices with their start and end apart: 7 -> 0, of which waited for: 7 -> 0; matrix products, arithmetic and copies ran while one was open for 14% -> 0% of each run, Pallas kernels for 0% -> 0%
where the time goes in v1:
time: 35.6 us; the launch traced here: 35.2 us
  Pallas kernels  26.3 us (74%)
  local copies, waits for them, and re-layouts  8.3 us (23%)
  between operations  0.66 us (2%)
    pallas_call x1, Pallas kernels, fused_device(): pl.pallas_call(functools.partial(fused_kernel, n_seq), out_shape=[jax.Sha...  26.3 us
    unnamed x16, local copies, waits for them, and re-layouts  8.3 us

profile of v1, /device:TPU:1, one launch (start us, length us, event | category | flops | bytes accessed | tf_op | source)
XLA Modules:
  0.0 35.2 jit_solution(5516246374316790171)
XLA Ops:
  0.6 0.0 copy-start.5
  0.6 0.6 %copy-done.5 = s32[1,2]{1,0:T(1,128)S(1)} copy-done((s32[1,2]{1,0:T(1,128)S(1)}, s32[1,2]{1,0:T(1,128)}, u32[]{:S(2)}) %copy-start.5) | copy-done | bytes 32
  1.3 0.0 copy-start
  1.3 1.2 %copy-done = bf16[1,128,4096]{2,1,0:T(8,128)(2,1)S(1)} copy-done((bf16[1,128,4096]{2,1,0:T(8,128)(2,1)S(1)}, bf16[1,128,4096]{2,1,0:T(8,128)(2,1)}, u32[]{:S(2)}) %copy-start) | copy-done | bytes 1048600
  2.5 0.0 copy-start.1
  2.5 1.2 %copy-done.1 = bf16[256,2048]{1,0:T(8,128)(2,1)S(1)} copy-done((bf16[256,2048]{1,0:T(8,128)(2,1)S(1)}, bf16[256,2048]{1,0:T(8,128)(2,1)}, u32[]{:S(2)}) %copy-start.1) | copy-done | bytes 1048600
  3.7 0.0 copy-start.2
  3.7 0.8 %copy-done.2 = bf16[1,128,256]{2,1,0:T(8,128)(2,1)S(1)} copy-done((bf16[1,128,256]{2,1,0:T(8,128)(2,1)S(1)}, bf16[1,128,256]{2,1,0:T(8,128)(2,1)}, u32[]{:S(2)}) %copy-start.2) | copy-done | bytes 65560
  4.6 0.0 copy-start.3
  4.6 0.8 %copy-done.3 = bf16[1,128,256]{2,1,0:T(8,128)(2,1)S(1)} copy-done((bf16[1,128,256]{2,1,0:T(8,128)(2,1)S(1)}, bf16[1,128,256]{2,1,0:T(8,128)(2,1)}, u32[]{:S(2)}) %copy-start.3) | copy-done | bytes 65560
  5.4 0.0 copy-start.4
  5.4 0.8 %copy-done.4 = bf16[1,128,256]{2,1,0:T(8,128)(2,1)S(1)} copy-done((bf16[1,128,256]{2,1,0:T(8,128)(2,1)S(1)}, bf16[1,128,256]{2,1,0:T(8,128)(2,1)}, u32[]{:S(2)}) %copy-start.4) | copy-done | bytes 65560
  6.3 26.3 %shard_map.93 = (bf16[128,256]{1,0:T(8,128)(2,1)S(1)}, bf16[128,256]{1,0:T(8,128)(2,1)S(1)}, bf16[128,256]{1,0:T(8,128)(2,1)S(1)}, f32[1024,128]{1,0:T(8,128)S(1)}) custom-call(s32[1,2]{1,0:T(1,128)S(1)} %copy-done.5, bf16[128,256]{1,0:T(8,128)(2,1)S(1)} %bitcast.8, bf16[128,256]{1,0:T(8,128)(2,1)S(1)} %bitcast.9, bf16[128,256]{1,0:T(8,128)(2,1)S(1)} %bitcast.10, ...), custom_call_target="tpu_custom_call" | custom-call | tf_op jit(solution)/shard_map/pallas_call | solution.py:360
  32.5 0.6 %copy.14 = bf16[1,128,256]{2,1,0:T(8,128)(2,1)} copy(bf16[1,128,256]{2,1,0:T(8,128)(2,1)S(1)} %bitcast.13) | data formatting | bytes 131072
  33.2 0.6 %copy.15 = bf16[1,128,256]{2,1,0:T(8,128)(2,1)} copy(bf16[1,128,256]{2,1,0:T(8,128)(2,1)S(1)} %bitcast.12) | data formatting | bytes 131072
  33.8 0.6 %copy.16 = bf16[1,128,256]{2,1,0:T(8,128)(2,1)} copy(bf16[1,128,256]{2,1,0:T(8,128)(2,1)S(1)} %bitcast.11) | data formatting | bytes 131072
  34.4 0.8 %copy.17 = f32[1024,128]{1,0:T(8,128)} copy(f32[1024,128]{1,0:T(8,128)S(1)} %get-tuple-element.19) | data formatting | bytes 1048576
Async XLA Ops:
  0.6 0.7 %copy-start.5 = (s32[1,2]{1,0:T(1,128)S(1)}, s32[1,2]{1,0:T(1,128)}, u32[]{:S(2)}) copy-start(s32[1,2]{1,0:T(1,128)} %flags_ref.1) | copy-start | bytes 28
  1.3 1.2 %copy-start = (bf16[1,128,4096]{2,1,0:T(8,128)(2,1)S(1)}, bf16[1,128,4096]{2,1,0:T(8,128)(2,1)}, u32[]{:S(2)}) copy-start(bf16[1,128,4096]{2,1,0:T(8,128)(2,1)} %param.9) | copy-start | bytes 3145732
  2.5 1.2 %copy-start.1 = (bf16[256,2048]{1,0:T(8,128)(2,1)S(1)}, bf16[256,2048]{1,0:T(8,128)(2,1)}, u32[]{:S(2)}) copy-start(bf16[256,2048]{1,0:T(8,128)(2,1)} %w_hbm.1) | copy-start | bytes 3145732
  3.7 0.8 %copy-start.2 = (bf16[1,128,256]{2,1,0:T(8,128)(2,1)S(1)}, bf16[1,128,256]{2,1,0:T(8,128)(2,1)}, u32[]{:S(2)}) copy-start(bf16[1,128,256]{2,1,0:T(8,128)(2,1)} %param.6) | copy-start | bytes 196612
  4.6 0.8 %copy-start.3 = (bf16[1,128,256]{2,1,0:T(8,128)(2,1)S(1)}, bf16[1,128,256]{2,1,0:T(8,128)(2,1)}, u32[]{:S(2)}) copy-start(bf16[1,128,256]{2,1,0:T(8,128)(2,1)} %param.7) | copy-start | bytes 196612
  5.4 0.8 %copy-start.4 = (bf16[1,128,256]{2,1,0:T(8,128)(2,1)S(1)}, bf16[1,128,256]{2,1,0:T(8,128)(2,1)}, u32[]{:S(2)}) copy-start(bf16[1,128,256]{2,1,0:T(8,128)(2,1)} %param.8) | copy-start | bytes 196612

commit v2 on v1

--- a/solution.py
+++ b/solution.py
@@ -134,6 +134,8 @@
     w_sem,
     go_send_sem,
     go_recv_sem,
+    pass_send_sem,
+    pass_recv_sem,
     att_send_sem,
     att_recv_sem,
     term_send_sem,
@@ -151,6 +153,10 @@
     me = lax.axis_index("seq")
     core = lax.axis_index("fsdp")
     other = 1 - core
+    head = lax.axis_index("head")
+    parity = head % 2
+    twin = head + 1 - 2 * parity
+    share = block // 2
 
     def peer(mask):
         out = me
@@ -187,7 +193,10 @@
     pl.semaphore_signal(
         barrier, inc=1, device_id={"fsdp": other}, device_id_type=pl.DeviceIdType.MESH
     )
-    pl.semaphore_wait(barrier, n_seq)
+    pl.semaphore_signal(
+        barrier, inc=1, device_id={"head": twin}, device_id_type=pl.DeviceIdType.MESH
+    )
+    pl.semaphore_wait(barrier, n_seq + 1)
 
     kv_copies = []
     for level in range(levels):
@@ -211,10 +220,12 @@
     for mask in range(1, n_seq):
         target = peer(mask)
         columns = pl.ds(pl.multiple_of(target * rows, 128), rows)
+        lines = pl.ds(pl.multiple_of(parity * share, 16), share)
+        landing = pl.ds(pl.multiple_of(mask * block + parity * share, 16), share)
         go_copies.append(
             remote(
-                go_hbm.at[:, columns],
-                go_all.at[pl.ds(mask * block, block)],
+                go_hbm.at[lines, columns],
+                go_all.at[landing],
                 go_send_sem.at[mask - 1],
                 go_recv_sem.at[mask - 1],
                 {"seq": target},
@@ -228,6 +239,18 @@
     own_columns = pl.ds(pl.multiple_of(core * half_d, 128), half_d)
     other_columns = pl.ds(pl.multiple_of(other * half_d, 128), half_d)
     grad_att = contract(go_buf[:, own_columns], w_all[0], ((1,), (1,)))
+    pass_copies = []
+    for mask in range(1, n_seq):
+        landing = pl.ds(pl.multiple_of(mask * block + parity * share, 16), share)
+        pass_copies.append(
+            remote(
+                go_all.at[landing],
+                go_all.at[landing],
+                pass_send_sem.at[mask - 1],
+                pass_recv_sem.at[mask - 1],
+                {"head": twin},
+            )
+        )
     go_all[pl.ds(0, block), :] = go_buf[:, pl.ds(pl.multiple_of(me * rows, 128), rows)]
 
     for copy in locals_[:3]:
@@ -271,6 +294,9 @@
     for copy in att_copies:
         copy.start()
 
+    for copy, onward in zip(go_copies, pass_copies):
+        copy.wait_recv()
+        onward.start()
     w_copy.wait_recv()
     grad_att = grad_att + contract(go_buf[:, other_columns], w_all[1], ((1,), (1,)))
     grad_att = grad_att.astype(jnp.bfloat16)
@@ -305,7 +331,7 @@
     for copy in term_copies:
         copy.start()
 
-    for copy in go_copies:
+    for copy in pass_copies:
         copy.wait_recv()
     for copy in att_copies:
         copy.wait_recv()
@@ -342,8 +368,19 @@
         span = slice(i * step, (i + 1) * step)
         copy.wait_recv()
         gw_ref[span, :] = gw_ref[span, :] + part_recv[i].astype(jnp.float32)
-    for copy in kv_copies + [w_copy] + go_copies + att_copies + term_copies + part_copies:
+    for copy in kv_copies + [w_copy] + go_copies + pass_copies + att_copies + term_copies + part_copies:
         copy.wait_send()
+
+
+def deliver(*refs):
+    sources, targets, sem = refs[:4], refs[4:8], refs[8]
+    copies = [
+        pltpu.make_async_copy(src, dst, sem.at[i]) for i, (src, dst) in enumerate(zip(sources, targets))
+    ]
+    for copy in copies:
+        copy.start()
+    for copy in copies:
+        copy.wait()
 
 
 def fused_device(n_seq, query, keys, values, grad_out, w_out, link_flags):
@@ -354,7 +391,7 @@
     shape = (block, width)
     half_w = width // 2
     vmem = pl.BlockSpec(memory_space=pltpu.VMEM)
-    anywhere = pl.BlockSpec(memory_space=pl.ANY)
+    anywhere = pl.BlockSpec(memory_space=pltpu.HBM)
     bf16 = jnp.bfloat16
     dma = pltpu.SemaphoreType.DMA
     outs = pl.pallas_call(
@@ -385,21 +422,30 @@
             dma((n_seq - 1,)),
             dma((n_seq - 1,)),
             dma((n_seq - 1,)),
+            dma((n_seq - 1,)),
+            dma((n_seq - 1,)),
             dma((levels,)),
             dma((levels,)),
             dma((chunks,)),
             dma((chunks,)),
         ],
         compiler_params=pltpu.CompilerParams(
-            collective_id=0, has_side_effects=True, vmem_limit_bytes=40 * 1024 * 1024
+            collective_id=0, has_side_effects=True, vmem_limit_bytes=60 * 1024 * 1024
         ),
     )(link_flags, query[0], keys[0], values[0], grad_out[0], w_out)
+    outs = pl.pallas_call(
+        deliver,
+        out_shape=[jax.ShapeDtypeStruct(out.shape, out.dtype) for out in outs],
+        in_specs=[pl.BlockSpec(memory_space=pltpu.VMEM)] * 4,
+        out_specs=[pl.BlockSpec(memory_space=pltpu.HBM)] * 4,
+        scratch_shapes=[dma((4,))],
+    )(*outs)
     return outs[0][None], outs[1][None], outs[2][None], outs[3]
 
 
-def per_device(n_seq, query, keys, values, grad_out, w_out, link_flags):
+def per_device(n_seq, n_head, query, keys, values, grad_out, w_out, link_flags):
     args = (query, keys, values, grad_out, w_out, link_flags)
-    if query.shape[0] == 1 and (D // n_seq) % 512 == 0 and query.shape[2] == 2 * HD:
+    if query.shape[0] == 1 and (D // n_seq) % 512 == 0 and query.shape[2] == 2 * HD and n_head % 2 == 0:
         return fused_device(n_seq, *args)
     return plain_device(*args)
 
@@ -420,5 +466,5 @@
         P("seq", ("head", "fsdp")),
     )
     return jax.shard_map(
-        functools.partial(per_device, mesh.shape["seq"]), mesh=mesh, in_specs=in_specs, out_specs=out_specs, check_vma=False
-    )
+        functools.partial(per_device, mesh.shape["seq"], mesh.shape["head"]), mesh=mesh, in_specs=in_specs, out_specs=out_specs, check_vma=False
+    )

time: 35.6 us -> 27.5 us (0.77)
  local copies, waits for them, and re-layouts: 8.3 us -> 0 us
  Pallas kernels: 26.3 us -> 26.7 us
    unnamed x16 -> x0, local copies, waits for them, and re-layouts: 8.3 us -> none
    pallas_call x0 -> x1, Pallas kernels: none -> 2.05 us  [fused_device(): pl.pallas_call(deliver, out_shape=[jax.ShapeDtypeStruct(out.shape, out.dt...]
    pallas_call x1, Pallas kernels: 26.3 us -> 24.6 us  [fused_device(): pl.pallas_call(functools.partial(fused_kernel, n_seq), out_shape=[jax.Sha...]
where the time goes in v2:
time: 27.5 us; the launch traced here: 27.3 us
  Pallas kernels  26.7 us (97%)
  between operations  0.64 us (2%)
    pallas_call x1, Pallas kernels, fused_device(): pl.pallas_call(functools.partial(fused_kernel, n_seq), out_shape=[jax.Sha...  24.6 us
    pallas_call x1, Pallas kernels, fused_device(): pl.pallas_call(deliver, out_shape=[jax.ShapeDtypeStruct(out.shape, out.dt...  2.05 us

profile of v2, /device:TPU:1, one launch (start us, length us, event | category | flops | bytes accessed | tf_op | source)
XLA Modules:
  0.0 27.3 jit_solution(16299029517586296243)
XLA Ops:
  0.6 24.6 %shard_map.93 = (bf16[128,256]{1,0:T(8,128)(2,1)}, bf16[128,256]{1,0:T(8,128)(2,1)}, bf16[128,256]{1,0:T(8,128)(2,1)}, f32[1024,128]{1,0:T(8,128)}) custom-call(s32[1,2]{1,0:T(1,128)} %flags_ref.1, bf16[128,256]{1,0:T(8,128)(2,1)} %bitcast.8, bf16[128,256]{1,0:T(8,128)(2,1)} %bitcast.9, bf16[128,256]{1,0:T(8,128)(2,1)} %bitcast.10, ...), custom_call_target="tpu_custom_call" | custom-call | tf_op jit(solution)/shard_map/pallas_call | solution.py:397
  25.3 2.0 %shard_map.94 = (bf16[128,256]{1,0:T(8,128)(2,1)}, bf16[128,256]{1,0:T(8,128)(2,1)}, bf16[128,256]{1,0:T(8,128)(2,1)}, f32[1024,128]{1,0:T(8,128)}) custom-call(bf16[128,256]{1,0:T(8,128)(2,1)} %get-tuple-element.12.refs_0_, bf16[128,256]{1,0:T(8,128)(2,1)} %get-tuple-element.13.refs_1_, bf16[128,256]{1,0:T(8,128)(2,1)} %get-tuple-element.14.refs_2_, ...), custom_call_target="tpu_custom_call" | custom-call | tf_op jit(solution)/shard_map/pallas_call | solution.py:436

commit v3 on v2

--- a/solution.py
+++ b/solution.py
@@ -111,10 +111,15 @@
     values_hbm,
     go_hbm,
     w_hbm,
+    gq_out,
+    gk_out,
+    gv_out,
+    gw_out,
     gq_ref,
     gk_ref,
     gv_ref,
     gw_ref,
+    out_sem,
     q_buf,
     k_all,
     v_all,
@@ -126,6 +131,7 @@
     term_recv,
     gk_acc,
     gv_acc,
+    gw_acc,
     part_send,
     part_recv,
     local_sem,
@@ -317,6 +323,8 @@
             term_send[level, 1, :, cols] = value_terms[part].astype(jnp.bfloat16)
         gq_ref[:, cols] = contract(grad_scores, k_all[:, cols], ((1,), (0,))).astype(jnp.bfloat16)
 
+    out_copies = [pltpu.make_async_copy(gq_ref, gq_out, out_sem.at[0])]
+    out_copies[0].start()
     term_copies = []
     for level in range(levels):
         term_copies.append(
@@ -331,16 +339,21 @@
     for copy in term_copies:
         copy.start()
 
-    for copy in pass_copies:
-        copy.wait_recv()
-    for copy in att_copies:
-        copy.wait_recv()
     chunks = part_send.shape[0]
     step = rows // chunks
+    for copy in pass_copies[:1] + att_copies[:1]:
+        copy.wait_recv()
+    first = slice(0, 2 * block)
+    second = slice(2 * block, n_seq * block)
+    for i in range(chunks):
+        span = slice(i * step, (i + 1) * step)
+        gw_acc[span, :] = contract(go_all[first, span], att_all[first], ((0,), (0,)))
+    for copy in pass_copies[1:] + att_copies[1:]:
+        copy.wait_recv()
     part_copies = []
     for i in range(chunks):
         span = slice(i * step, (i + 1) * step)
-        product = contract(go_all[:, span], att_all[...], ((0,), (0,)))
+        product = gw_acc[span, :] + contract(go_all[second, span], att_all[second], ((0,), (0,)))
         low_half, high_half = product[:, :half_w], product[:, half_w:]
         part_send[i] = jnp.where(core == 0, high_half, low_half).astype(jnp.bfloat16)
         copy = remote(
@@ -363,13 +376,24 @@
         grad_value = grad_value + term_recv[level, 1].astype(jnp.float32)
     gk_ref[...] = grad_key.astype(jnp.bfloat16)
     gv_ref[...] = grad_value.astype(jnp.bfloat16)
+    out_copies.append(pltpu.make_async_copy(gk_ref, gk_out, out_sem.at[1]))
+    out_copies.append(pltpu.make_async_copy(gv_ref, gv_out, out_sem.at[2]))
+    out_copies[1].start()
+    out_copies[2].start()
 
     for i, copy in enumerate(part_copies):
         span = slice(i * step, (i + 1) * step)
         copy.wait_recv()
         gw_ref[span, :] = gw_ref[span, :] + part_recv[i].astype(jnp.float32)
+        out_copy = pltpu.make_async_copy(
+            gw_ref.at[pl.ds(i * step, step)], gw_out.at[pl.ds(i * step, step)], out_sem.at[3 + i]
+        )
+        out_copy.start()
+        out_copies.append(out_copy)
     for copy in kv_copies + [w_copy] + go_copies + pass_copies + att_copies + term_copies + part_copies:
         copy.wait_send()
+    for copy in out_copies:
+        copy.wait()
 
 
 def deliver(*refs):
@@ -387,10 +411,9 @@
     _, block, width = query.shape
     levels = n_seq.bit_length() - 1
     rows = D // n_seq
-    chunks = 4
+    chunks = 2
     shape = (block, width)
     half_w = width // 2
-    vmem = pl.BlockSpec(memory_space=pltpu.VMEM)
     anywhere = pl.BlockSpec(memory_space=pltpu.HBM)
     bf16 = jnp.bfloat16
     dma = pltpu.SemaphoreType.DMA
@@ -399,8 +422,13 @@
         out_shape=[jax.ShapeDtypeStruct(shape, bf16)] * 3
         + [jax.ShapeDtypeStruct((rows, half_w), jnp.float32)],
         in_specs=[pl.BlockSpec(memory_space=pltpu.SMEM)] + [anywhere] * 5,
-        out_specs=[vmem] * 4,
+        out_specs=[pl.BlockSpec(memory_space=pltpu.HBM)] * 4,
         scratch_shapes=[
+            pltpu.VMEM(shape, bf16),
+            pltpu.VMEM(shape, bf16),
+            pltpu.VMEM(shape, bf16),
+            pltpu.VMEM((rows, half_w), jnp.float32),
+            dma((3 + chunks,)),
             pltpu.VMEM(shape, bf16),
             pltpu.VMEM(((levels + 1) * block, width), bf16),
             pltpu.VMEM(((levels + 1) * block, width), bf16),
@@ -412,6 +440,7 @@
             pltpu.VMEM((levels, 2) + shape, bf16),
             pltpu.VMEM(shape, jnp.float32),
             pltpu.VMEM(shape, jnp.float32),
+            pltpu.VMEM((rows, width), jnp.float32),
             pltpu.VMEM((chunks, rows // chunks, half_w), bf16),
             pltpu.VMEM((chunks, rows // chunks, half_w), bf16),
             dma((5,)),

time: 27.5 us -> 26.8 us (0.975)
  Pallas kernels: 26.7 us -> 26 us
    pallas_call x1, Pallas kernels: 24.6 us -> 23.9 us  [fused_device(): pl.pallas_call(functools.partial(fused_kernel, n_seq), out_shape=[jax.Sha...]
where the time goes in v3:
time: 26.8 us; the launch traced here: 26.6 us
  Pallas kernels  26 us (97%)
  between operations  0.64 us (2%)
    pallas_call x1, Pallas kernels, fused_device(): pl.pallas_call(functools.partial(fused_kernel, n_seq), out_shape=[jax.Sha...  23.9 us
    pallas_call x1, Pallas kernels, fused_device(): pl.pallas_call(deliver, out_shape=[jax.ShapeDtypeStruct(out.shape, out.dt...  2.05 us

profile of v3, /device:TPU:1, one launch (start us, length us, event | category | flops | bytes accessed | tf_op | source)
XLA Modules:
  0.0 26.6 jit_solution(13003162072412905355)
XLA Ops:
  0.6 23.9 %shard_map.93 = (bf16[128,256]{1,0:T(8,128)(2,1)}, bf16[128,256]{1,0:T(8,128)(2,1)}, bf16[128,256]{1,0:T(8,128)(2,1)}, f32[1024,128]{1,0:T(8,128)}) custom-call(s32[1,2]{1,0:T(1,128)} %flags_ref.1, bf16[128,256]{1,0:T(8,128)(2,1)} %bitcast.8, bf16[128,256]{1,0:T(8,128)(2,1)} %bitcast.9, bf16[128,256]{1,0:T(8,128)(2,1)} %bitcast.10, ...), custom_call_target="tpu_custom_call" | custom-call | tf_op jit(solution)/shard_map/pallas_call | solution.py:420
  24.6 2.0 %shard_map.94 = (bf16[128,256]{1,0:T(8,128)(2,1)}, bf16[128,256]{1,0:T(8,128)(2,1)}, bf16[128,256]{1,0:T(8,128)(2,1)}, f32[1024,128]{1,0:T(8,128)}) custom-call(bf16[128,256]{1,0:T(8,128)(2,1)} %get-tuple-element.12.refs_0_, bf16[128,256]{1,0:T(8,128)(2,1)} %get-tuple-element.13.refs_1_, bf16[128,256]{1,0:T(8,128)(2,1)} %get-tuple-element.14.refs_2_, ...), custom_call_target="tpu_custom_call" | custom-call | tf_op jit(solution)/shard_map/pallas_call | solution.py:465
